TPU v7x, 256 devices: a whole 4x4x8 slice. The times are simulated.
256 devices in a mesh: replica: 16 (over y, x_lo, core), fsdp: 16 (over z, x_hi).
Axes of the slice: x: 4 (x_hi: 2, x_lo: 2; x = x_hi * 2 + x_lo), y: 4, z: 8, core: 2. Of those that a mesh axis runs over, the one named last changes fastest.
Arguments:
- hidden_in: bfloat16 [16, 4096, 3584], P('replica', 'fsdp'), may hold values from -6 to 6
- local_weights: bfloat16 [16, 3584, 2048], P('replica', 'fsdp'), may hold values from -6 to 6
- cotangent: bfloat16 [16, 4096, 2048], P('replica', 'fsdp'), may hold values from -6 to 6
- global_weights: float32 [3584, 2048], P('fsdp'), may hold values from -6 to 6
- outer_momentum: float32 [3584, 2048], P('fsdp'), may hold values from -3 to 3
- step_index: int32 [1], replicated, may hold values from 0 to 1023
Outputs:
- projected: bfloat16 [16, 4096, 2048], P('replica', 'fsdp')
- input_grad: bfloat16 [16, 4096, 3584], P('replica', 'fsdp')
- new_weights: bfloat16 [16, 3584, 2048], P('replica', 'fsdp')
- new_global: float32 [3584, 512], P('fsdp')
- new_momentum: float32 [3584, 512], P('fsdp')
All inputs are finite; a program needn't handle non-finite values.
Results may differ from a plain program's by a relative error of at most 0.013.
Values may be sent and summed in bfloat16 or wider, within the bound.
A program may use at most 128 MiB of HBM per device.

v0:
```python
import math

import jax
import jax.numpy as jnp
from jax import lax
from jax.sharding import PartitionSpec as P

KVW = 2048
FRAGS = 4


EPSILON = 1e-05
INNER_RATE = 0.25
OUTER_RATE = 0.7
NESTEROV = 0.9
MIX_KEEP = 0.5


def outer_update(global_part, moment_part, mean_part):
    delta = global_part - mean_part
    moment_next = NESTEROV * moment_part + delta
    global_next = global_part - OUTER_RATE * (delta + NESTEROV * moment_next)
    return (global_next, moment_next)


def body(hidden_in, local_weights, cotangent, global_weights, outer_momentum, step_index):
    features = hidden_in.shape[2]
    scale = 1.0 / math.sqrt(features)
    frag_cols = KVW // FRAGS
    wide = hidden_in[0].astype(jnp.float32)
    rms = jnp.sqrt(jnp.mean(wide * wide, -1, keepdims=True) + EPSILON)
    exact = wide / rms
    normed = exact.astype(jnp.bfloat16)
    grads_in = cotangent[0]
    full_weights = lax.all_gather(local_weights[0], "fsdp", axis=0, tiled=True)
    projected = (jnp.dot(normed, full_weights, preferred_element_type=jnp.float32) * scale).astype(
        jnp.bfloat16
    )
    back = (
        lax.dot_general(
            grads_in, full_weights, (((1,), (1,)), ((), ())), preferred_element_type=jnp.float32
        )
        * scale
    )
    input_grad = ((back - exact * jnp.mean(back * exact, -1, keepdims=True)) / rms).astype(
        jnp.bfloat16
    )
    gradient = lax.psum_scatter(
        (
            lax.dot_general(
                normed, grads_in, (((0,), (0,)), ((), ())), preferred_element_type=jnp.float32
            )
            * scale
        ).astype(jnp.bfloat16),
        "fsdp",
        scatter_dimension=0,
        tiled=True,
    ).astype(jnp.float32)
    own_weights = local_weights[0].astype(jnp.float32)
    updated = own_weights - INNER_RATE * gradient
    start = step_index[0] % FRAGS * frag_cols
    local_frag = lax.dynamic_slice_in_dim(own_weights, start, frag_cols, 1)
    global_frag = lax.dynamic_slice_in_dim(global_weights, start, frag_cols, 1)
    moment_frag = lax.dynamic_slice_in_dim(outer_momentum, start, frag_cols, 1)
    replicas = lax.axis_size("replica")
    total = lax.psum(local_frag.astype(jnp.bfloat16), "replica").astype(jnp.float32)
    new_global, new_momentum = outer_update(global_frag, moment_frag, total / replicas)
    upd_frag = lax.dynamic_slice_in_dim(updated, start, frag_cols, 1)
    mixed = MIX_KEEP * upd_frag + (1.0 - MIX_KEEP) * new_global
    new_weights = lax.dynamic_update_slice_in_dim(updated, mixed, start, 1).astype(jnp.bfloat16)
    return (projected[None], input_grad[None], new_weights[None], new_global, new_momentum)


def solution(mesh):
    placed = (
        P("replica", "fsdp", None),
        P("replica", "fsdp", None),
        P("replica", "fsdp", None),
        P("fsdp", None),
        P("fsdp", None),
        P(),
    )
    return jax.shard_map(
        body,
        mesh=mesh,
        in_specs=placed,
        out_specs=(
            P("replica", "fsdp", None),
            P("replica", "fsdp", None),
            P("replica", "fsdp", None),
            P("fsdp", None),
            P("fsdp", None),
        ),
        check_vma=False,
    )
```

profile of v0, /device:TPU:2, one launch (start us, length us, event | category | flops | bytes accessed | tf_op | source)
XLA Modules:
  0.0 500.0 jit_solution(1808210386668709378)
XLA Ops:
  8.0 0.0 copy-start
  8.0 0.0 all-gather.3.cloned.1.call-start
  8.1 0.7 all-gather.3.cloned.1.call-update
  8.7 0.0 reduce-scatter.2.cloned.1.call-start
  8.8 1.9 fusion.9
  10.7 0.0 copy-done
  10.8 9.0 %multiply_convert_fusion = bf16[3584,2048]{1,0:T(8,128)(2,1)} fusion(bf16[1,256,3584]{2,1,0:T(8,128)(2,1)} %param.6, f32[256]{0:T(256)S(1)} %add_sqrt_fusion, bf16[1,256,2048]{2,1,0:T(8,128)(2,1)S(1)} %copy-done), kind=kOutput, calls=%fused_computation | convolution fusion | flops 3775528960 | bytes 17564672 | tf_op jit(solution)/shard_map/dot_general | solution.py:50
  19.7 0.0 copy-start.1
  19.7 0.0 reduce-scatter.2.cloned.1.call-update
  19.8 0.0 all-reduce.2.cloned.1.call-start
  20.6 1.6 fusion.27
  22.3 0.0 all-reduce.2.cloned.1.call-update
  22.3 192.9 %all-gather.3.cloned.1.call-done = bf16[1,3584,2048]{2,1,0:T(8,128)(2,1)} async-done(((bf16[1,224,2048]{2,1,0:T(8,128)(2,1)}), bf16[1,3584,2048]{2,1,0:T(8,128)(2,1)}) %all-gather.3.cloned.1.call-update) | async-done | bytes 14680080 | tf_op jit(solution)/shard_map/all_gather | solution.py:35
  215.1 0.0 copy-done.1
  215.1 11.1 %multiply_reduce_fusion = (f32[256]{0:T(256)S(1)}, f32[256,3584]{1,0:T(8,128)}) fusion(f32[256]{0:T(256)S(1)} %add_sqrt_fusion, bf16[1,256,3584]{2,1,0:T(8,128)(2,1)S(1)} %copy-done.1, bf16[1,3584,2048]{2,1,0:T(8,128)(2,1)} %all-gather.3.cloned.1.call-done, bf16[1,256,2048]{2,1,0:T(8,128)(2,1)S(1)} %copy-done), kind=kOutput, calls=%fused_computation.13 | convolution fusion | flops 3762683648 | bytes 21235712 | tf_op jit(solution)/shard_map/dot_general | solution.py:40
  226.3 4.2 fusion.24
  230.5 8.5 %fusion.17 = bf16[1,256,2048]{2,1,0:T(8,128)(2,1)} fusion(bf16[1,3584,2048]{2,1,0:T(8,128)(2,1)} %all-gather.3.cloned.1.call-done, bf16[1,256,3584]{2,1,0:T(8,128)(2,1)S(1)} %copy-done.1, f32[256]{0:T(256)S(1)} %add_sqrt_fusion), kind=kOutput, calls=%fused_computation.16 | convolution fusion | flops 3761897472 | bytes 17564672 | tf_op jit(solution)/shard_map/dot_general | solution.py:36
  239.0 248.2 %reduce-scatter.2.cloned.1.call-done = bf16[224,2048]{1,0:T(8,128)(2,1)} async-done(((bf16[3584,2048]{1,0:T(8,128)(2,1)}), bf16[224,2048]{1,0:T(8,128)(2,1)}) %reduce-scatter.2.cloned.1.call-update) | async-done | bytes 917520 | tf_op jit(solution)/shard_map/reduce_scatter | solution.py:48
  487.3 1.8 bitcast_subtract_fusion
  489.0 0.0 all-reduce.2.cloned.1.call-done
  489.1 2.4 multiply_dynamic-update-slice_fusion
  491.5 1.0 convert_bitcast_fusion.1
  (2 shorter events, 0.0 us)
Async XLA Ops:
  8.0 2.8 copy-start
  8.0 207.1 %all-gather.3.cloned.1.call-start = ((), (), s32[]{:S(2)}) async-start(), calls=%async_computation.3 | async-start | bytes 15597568 | tf_op jit(solution)/shard_map/all_gather | solution.py:35
  8.7 478.5 %reduce-scatter.2.cloned.1.call-start = ((), (), s32[]{:S(2)}) async-start(), calls=%async_computation.1 | async-start | bytes 15597568 | tf_op jit(solution)/shard_map/reduce_scatter | solution.py:48
  19.7 195.4 %copy-start.1 = (bf16[1,256,3584]{2,1,0:T(8,128)(2,1)S(1)}, bf16[1,256,3584]{2,1,0:T(8,128)(2,1)}, u32[]{:S(2)}) copy-start(bf16[1,256,3584]{2,1,0:T(8,128)(2,1)} %param.6) | copy-start | bytes 5505028
  19.8 469.3 %all-reduce.2.cloned.1.call-start = ((), (), s32[]{:S(2)}) async-start(), calls=%async_computation.2 | async-start | bytes 458752 | tf_op jit(solution)/shard_map/psum | solution.py:66
Sparse Core Ops, SparseCore 0:
  11.4 203.6 all-gather.2
  219.3 267.9 reduce-scatter.1
Sparse Core Ops, SparseCore 1:
  23.6 197.8 all-reduce.1
where the time goes:
time: 502 us; the launch traced here: 500 us
  waiting for transfers between devices  442 us (88%)
  matrix products  28.6 us (6%)
  between operations  16.3 us (3%)
  other arithmetic  11.4 us (2%)
    reduce_scatter x1, waiting for transfers between devices, body(): lax.psum_scatter((lax.dot_general(normed, grads_in, (((0,), (0,)), ((), (...  248 us
    all_gather x1, waiting for transfers between devices, body(): full_weights = lax.all_gather(local_weights[0], 'fsdp', axis=0, tiled=True)  193 us
    dot_general x1, matrix products, body(): lax.dot_general(grads_in, full_weights, (((1,), (1,)), ((), ())), preferr...  11.1 us
  transfers between devices with their start and end apart: 3, of which 2 were waited for; matrix products, arithmetic and copies ran while one was open for 8% of the time, Pallas kernels for 0%

commit v1 on v0

v1 whole, which is shorter than its diff:
```python
import functools
import math

import jax
import jax.numpy as jnp
from jax import lax
from jax.experimental import pallas as pl
from jax.experimental.pallas import tpu as pltpu
from jax.sharding import PartitionSpec as P

KVW = 2048
FRAGS = 4
DW = 3584
HALF = DW // 2
TOK = 256
ROWS = 224
SIDE = ROWS // 2
NZ = 8
PARTS = 2
WIDE = KVW // PARTS
SCALE = 1.0 / math.sqrt(DW)

EPSILON = 1e-05
INNER_RATE = 0.25
OUTER_RATE = 0.7
NESTEROV = 0.9
MIX_KEEP = 0.5

MESH = pl.DeviceIdType.MESH
F32 = jnp.float32
BF16 = jnp.bfloat16


def outer_update(global_part, moment_part, mean_part):
    delta = global_part - mean_part
    moment_next = NESTEROV * moment_part + delta
    global_next = global_part - OUTER_RATE * (delta + NESTEROV * moment_next)
    return (global_next, moment_next)


def dot_nn(a, b):
    return jnp.dot(a, b, preferred_element_type=F32)


def dot_nt(a, b):
    return lax.dot_general(a, b, (((1,), (1,)), ((), ())), preferred_element_type=F32)


def chunk(i, size):
    return pl.ds(pl.multiple_of(i * size, size), size)


def kernel(
    hid_in, w_in, g_in, proj_out, ig_out, grad_out,
    hid, g_own, g_far, ht, n_halves, n_far, n_rows, wg, grads, ring,
    back_own, back_send, back_far, p_own, p_send, p_far, igt, ig_rows, p_rows,
    ag_send, ag_recv, rs_send, rs_recv, x_send, x_recv, local,
):
    replica = lax.axis_index("replica")
    place = lax.axis_index("fsdp")
    z, side = place // 2, lax.rem(place, 2)
    up = (replica, lax.rem(z + 1, NZ) * 2 + side)
    down = (replica, lax.rem(z + NZ - 1, NZ) * 2 + side)
    partner = (replica, z * 2 + 1 - side)

    def half_rows(block, d):
        return pl.ds(pl.multiple_of(block * ROWS + d * SIDE, 16), SIDE)

    def ring_block(step, d):
        return lax.rem(z - step + 2 * NZ, NZ) if d == 0 else lax.rem(z + step, NZ)

    load_hid = pltpu.make_async_copy(hid_in, hid, local.at[0])
    load_g = pltpu.make_async_copy(g_in, g_own, local.at[1])
    load_w = pltpu.make_async_copy(
        w_in, wg.at[pl.ds(pl.multiple_of(z * ROWS, 16), ROWS)], local.at[2]
    )
    load_hid.start()
    load_g.start()
    load_w.start()

    barrier = pltpu.get_barrier_semaphore()
    for other in (up, down, partner):
        pl.semaphore_signal(barrier, inc=1, device_id=other, device_id_type=MESH)
    pl.semaphore_wait(barrier, 3)

    def gather_copy(step, d):
        rows = half_rows(ring_block(step, d), d)
        return pltpu.make_async_remote_copy(
            src_ref=w_in.at[pl.ds(d * SIDE, SIDE)] if step == 0 else wg.at[rows],
            dst_ref=wg.at[rows],
            send_sem=ag_send.at[d, step],
            recv_sem=ag_recv.at[d, step],
            device_id=up if d == 0 else down,
            device_id_type=MESH,
        )

    def swap(src, dst, i):
        return pltpu.make_async_remote_copy(
            src_ref=src, dst_ref=dst, send_sem=x_send.at[i], recv_sem=x_recv.at[i],
            device_id=partner, device_id_type=MESH,
        )

    gathers = {}

    def gather_step(step):
        for d in range(2):
            if step > 0:
                gathers[step - 1, d].wait_recv()
            if step < NZ - 1:
                gathers[step, d] = gather_copy(step, d)
                gathers[step, d].start()

    sums = {}

    def sum_step(step):
        for part in range(PARTS):
            cols = pl.ds(part * WIDE, WIDE)
            for d in range(2):
                block = ring_block(step + 1, d)
                rows = half_rows(block, d)
                if step == 0:
                    src = grads.at[rows, cols]
                else:
                    sums[step - 1, d, part].wait_recv()
                    slot = ring.at[d, step - 1, :, cols]
                    total = grads[rows, cols].astype(F32) + slot[...].astype(F32)
                    if step == NZ - 1:
                        grad_out[pl.ds(d * SIDE, SIDE), cols] = total
                        continue
                    slot[...] = total.astype(BF16)
                    src = slot
                sums[step, d, part] = pltpu.make_async_remote_copy(
                    src_ref=src,
                    dst_ref=ring.at[d, step, :, cols],
                    send_sem=rs_send.at[d, part, step],
                    recv_sem=rs_recv.at[d, part, step],
                    device_id=up if d == 0 else down,
                    device_id_type=MESH,
                )
                sums[step, d, part].start()

    gather_step(0)
    send_g = swap(g_in, g_far, 0)
    send_g.start()

    load_hid.wait()

    def turn(i, squares):
        tile = hid[:, chunk(i, 256)].astype(F32).T
        ht[chunk(i, 256), :] = tile.astype(BF16)
        return squares + jnp.sum(tile * tile, 0, keepdims=True)

    squares = lax.fori_loop(0, DW // 256, turn, jnp.zeros((1, TOK), F32))
    inverse = 1.0 / jnp.sqrt(squares * (1.0 / DW) + EPSILON)

    def normalise(i, _):
        for d in range(2):
            rows = pl.ds(pl.multiple_of((2 * i + d) * ROWS, 16), ROWS)
            n_halves[d, pl.ds(pl.multiple_of(i * ROWS, 16), ROWS), :] = (
                ht[rows, :].astype(F32) * inverse
            ).astype(BF16)
        return 0

    lax.fori_loop(0, NZ, normalise, 0)
    send_n = swap(n_halves.at[1 - side], n_far, 1)
    send_n.start()

    load_g.wait()
    load_w.wait()
    for step in range(1, 6):
        gather_step(step)

    send_g.wait_recv()
    send_n.wait_recv()

    def gradient_tile(i, _):
        rows = chunk(i, 256)
        a, b = n_halves[side, rows, :], n_far[rows, :]
        for part in range(4):
            cols = pl.ds(part * 512, 512)
            term = dot_nn(a, g_own[:, cols]) + dot_nn(b, g_far[:, cols])
            grads[rows, cols] = (term * SCALE).astype(BF16)
        return 0

    lax.fori_loop(0, HALF // 256, gradient_tile, 0)
    gather_step(6)
    sum_step(0)

    def rows_of(i, _):
        rows = chunk(i, 256)
        n_rows[0, :, rows] = n_halves[side, rows, :].astype(F32).T.astype(BF16)
        n_rows[1, :, rows] = n_far[rows, :].astype(F32).T.astype(BF16)
        return 0

    lax.fori_loop(0, HALF // 256, rows_of, 0)
    gather_step(7)

    def back_tile(far):
        def run(i, _):
            rows = chunk(i, 256)
            if far:
                back_send[rows, :] = (dot_nt(wg[rows, :], g_far[...]) * SCALE).astype(BF16)
            else:
                back_own[rows, :] = dot_nt(wg[rows, :], g_own[...]) * SCALE
            return 0

        lax.fori_loop(0, HALF // 256, run, 0)

    def project_tile(far):
        def run(i, _):
            cols = chunk(i, 512)
            if far:
                p_send[:, cols] = (dot_nn(n_rows[1], wg[:, cols]) * SCALE).astype(BF16)
            else:
                p_own[:, cols] = dot_nn(n_rows[0], wg[:, cols]) * SCALE
            return 0

        lax.fori_loop(0, KVW // 512, run, 0)

    back_tile(True)
    send_back = swap(back_send, back_far, 2)
    send_back.start()
    sum_step(1)
    project_tile(True)
    send_p = swap(p_send, p_far, 3)
    send_p.start()
    sum_step(2)
    back_tile(False)
    sum_step(3)
    project_tile(False)
    sum_step(4)

    send_back.wait_recv()

    def row_pair(i):
        kept = pl.ds(pl.multiple_of(i * ROWS, 16), ROWS)
        own = pl.ds(pl.multiple_of((2 * i + side) * ROWS, 16), ROWS)
        other = pl.ds(pl.multiple_of((2 * i + 1 - side) * ROWS, 16), ROWS)
        return ((back_own[kept, :], own), (back_far[kept, :].astype(F32), other))

    def overlap(i, total):
        for back, rows in row_pair(i):
            total = total + jnp.sum(back * ht[rows, :].astype(F32), 0, keepdims=True)
        return total

    total = lax.fori_loop(0, NZ, overlap, jnp.zeros((1, TOK), F32))
    factor = total * inverse * inverse * (1.0 / DW)

    def back_norm(i, _):
        for back, rows in row_pair(i):
            igt[rows, :] = (back - ht[rows, :].astype(F32) * factor) * inverse
        return 0

    lax.fori_loop(0, NZ, back_norm, 0)

    def turn_back(i, _):
        ig_rows[:, chunk(i, 256)] = igt[chunk(i, 256), :].T.astype(BF16)
        return 0

    lax.fori_loop(0, DW // 256, turn_back, 0)
    store_ig = pltpu.make_async_copy(ig_rows, ig_out, local.at[3])
    store_ig.start()
    sum_step(5)

    send_p.wait_recv()

    def finish(i, _):
        cols = chunk(i, 512)
        p_rows[:, cols] = (p_own[:, cols] + p_far[:, cols].astype(F32)).astype(BF16)
        return 0

    lax.fori_loop(0, KVW // 512, finish, 0)
    store_p = pltpu.make_async_copy(p_rows, proj_out, local.at[4])
    store_p.start()
    sum_step(6)
    sum_step(7)

    store_ig.wait()
    store_p.wait()
    for copy in (send_g, send_n, send_back, send_p):
        copy.wait_send()
    for copy in gathers.values():
        copy.wait_send()
    for copy in sums.values():
        copy.wait_send()


def step_kernel(hidden, weights, cot):
    anywhere = pl.BlockSpec(memory_space=pl.ANY)
    vmem = pltpu.VMEM
    return pl.pallas_call(
        kernel,
        out_shape=(
            jax.ShapeDtypeStruct((TOK, KVW), BF16),
            jax.ShapeDtypeStruct((TOK, DW), BF16),
            jax.ShapeDtypeStruct((ROWS, KVW), F32),
        ),
        in_specs=[anywhere] * 3,
        out_specs=(anywhere, anywhere, pl.BlockSpec(memory_space=pltpu.VMEM)),
        scratch_shapes=[
            vmem((TOK, DW), BF16),
            vmem((TOK, KVW), BF16),
            vmem((TOK, KVW), BF16),
            vmem((DW, TOK), BF16),
            vmem((2, HALF, TOK), BF16),
            vmem((HALF, TOK), BF16),
            vmem((2, TOK, HALF), BF16),
            vmem((HALF, KVW), BF16),
            vmem((HALF, KVW), BF16),
            vmem((2, NZ - 1, SIDE, KVW), BF16),
            vmem((HALF, TOK), F32),
            vmem((HALF, TOK), BF16),
            vmem((HALF, TOK), BF16),
            vmem((TOK, KVW), F32),
            vmem((TOK, KVW), BF16),
            vmem((TOK, KVW), BF16),
            vmem((DW, TOK), F32),
            vmem((TOK, DW), BF16),
            vmem((TOK, KVW), BF16),
            pltpu.SemaphoreType.DMA((2, NZ - 1)),
            pltpu.SemaphoreType.DMA((2, NZ - 1)),
            pltpu.SemaphoreType.DMA((2, PARTS, NZ - 1)),
            pltpu.SemaphoreType.DMA((2, PARTS, NZ - 1)),
            pltpu.SemaphoreType.DMA((4,)),
            pltpu.SemaphoreType.DMA((4,)),
            pltpu.SemaphoreType.DMA((5,)),
        ],
        compiler_params=pltpu.CompilerParams(
            collective_id=0, has_side_effects=True, vmem_limit_bytes=56 << 20
        ),
        cost_estimate=pl.CostEstimate(
            flops=6 * TOK * DW * KVW, bytes_accessed=600 << 20, transcendentals=0
        ),
    )(hidden, weights, cot)


def body(hidden_in, local_weights, cotangent, global_weights, outer_momentum, step_index):
    frag_cols = KVW // FRAGS
    start = step_index[0] % FRAGS * frag_cols
    local_frag = lax.dynamic_slice_in_dim(local_weights[0], start, frag_cols, 1)
    replicas = lax.axis_size("replica")
    total = lax.psum(local_frag, "replica").astype(F32)
    projected, input_grad, gradient = step_kernel(hidden_in[0], local_weights[0], cotangent[0])
    global_frag = lax.dynamic_slice_in_dim(global_weights, start, frag_cols, 1)
    moment_frag = lax.dynamic_slice_in_dim(outer_momentum, start, frag_cols, 1)
    new_global, new_momentum = outer_update(global_frag, moment_frag, total / replicas)
    updated = local_weights[0].astype(F32) - INNER_RATE * gradient
    upd_frag = lax.dynamic_slice_in_dim(updated, start, frag_cols, 1)
    mixed = MIX_KEEP * upd_frag + (1.0 - MIX_KEEP) * new_global
    new_weights = lax.dynamic_update_slice_in_dim(updated, mixed, start, 1).astype(BF16)
    return (projected[None], input_grad[None], new_weights[None], new_global, new_momentum)


def solution(mesh):
    placed = (
        P("replica", "fsdp", None),
        P("replica", "fsdp", None),
        P("replica", "fsdp", None),
        P("fsdp", None),
        P("fsdp", None),
        P(),
    )
    return jax.shard_map(
        body,
        mesh=mesh,
        in_specs=placed,
        out_specs=(
            P("replica", "fsdp", None),
            P("replica", "fsdp", None),
            P("replica", "fsdp", None),
            P("fsdp", None),
            P("fsdp", None),
        ),
        check_vma=False,
    )
```

time: 502 us -> 175 us (0.35)
  waiting for transfers between devices: 442 us -> 0.04 us
  Pallas kernels: 0 us -> 150 us
  matrix products: 28.6 us -> 0 us
  other arithmetic: 11.4 us -> 5.21 us
    reduce_scatter x1 -> x0, waiting for transfers between devices: 248 us -> none  [body(): lax.psum_scatter((lax.dot_general(normed, grads_in, (((0,), (0,)), ((), (...]
    all_gather x1 -> x0, waiting for transfers between devices: 193 us -> none  [body(): full_weights = lax.all_gather(local_weights[0], 'fsdp', axis=0, tiled=True)]
    pallas_call x0 -> x1, Pallas kernels: none -> 150 us  [step_kernel(): pl.pallas_call(kernel, out_shape=(jax.ShapeDtypeStruct((TOK, KVW), BF16),...]
    dot_general x3 -> x0, matrix products: 28.6 us -> none  [the longest x1 11.1 us: body(): lax.dot_general(grads_in, full_weights, (((1,), (1,)), ((), ())), preferr...]
  transfers between devices with their start and end apart: 3 -> 1, of which waited for: 2 -> 0; matrix products, arithmetic and copies ran while one was open for 8% -> 1% of each run, Pallas kernels for 0% -> 86%
where the time goes in v1:
time: 175 us; the launch traced here: 174 us
  Pallas kernels  150 us (86%)
  between operations  14.7 us (8%)
  other arithmetic  5.21 us (3%)
  local copies, waits for them, and re-layouts  4.36 us (2%)
    pallas_call x1, Pallas kernels, step_kernel(): pl.pallas_call(kernel, out_shape=(jax.ShapeDtypeStruct((TOK, KVW), BF16),...  150 us
  transfers between devices with their start and end apart: 1, of which 0 were waited for; matrix products, arithmetic and copies ran while one was open for 1% of the time, Pallas kernels for 86%

profile of v1, /device:TPU:2, one launch (start us, length us, event | category | flops | bytes accessed | tf_op | source)
XLA Modules:
  0.0 174.2 jit_solution(13133412482451532881)
XLA Ops:
  7.2 0.0 all-reduce.2.cloned.1.call-start
  7.9 1.6 dynamic-slice_bitcast_fusion
  9.5 0.0 all-reduce.2.cloned.1.call-update
  9.5 0.0 copy-start.1
  9.6 149.8 %shard_map.101 = (bf16[256,2048]{1,0:T(8,128)(2,1)}, bf16[256,3584]{1,0:T(8,128)(2,1)}, f32[224,2048]{1,0:T(8,128)}) custom-call(bf16[256,3584]{1,0:T(8,128)(2,1)} %bitcast.17, bf16[224,2048]{1,0:T(8,128)(2,1)} %bitcast.15, bf16[256,2048]{1,0:T(8,128)(2,1)} %bitcast.18), custom_call_target="tpu_custom_call" | custom-call | flops 11274289152 | bytes 629145600 | tf_op jit(solution)/shard_map/pallas_call | solution.py:291
  159.4 0.0 copy-done.1
  159.4 1.7 multiply_subtract_fusion
  161.1 0.0 all-reduce.2.cloned.1.call-done
  161.2 2.4 %multiply_dynamic-update-slice_fusion = (f32[224,2048]{1,0:T(8,128)S(1)}, f32[224,512]{1,0:T(8,128)}, f32[224,512]{1,0:T(8,128)}) fusion(f32[224,2048]{1,0:T(8,128)S(1)} %multiply_subtract_fusion, s32[]{:T(128)S(6)} %select_n.15, bf16[224,512]{1,0:T(8,128)(2,1)} %all-reduce.2.cloned.1.call-done, f32[224,2048]{1,0:T(8,128)} %param.9, f32[224,2048]{1,0:T(8,128)} %param.10), kind=kLoop, calls=%fused_computation.2 | loop fusion | flops 1261568 | bytes 2981892 | tf_op jit(solution)/shard_map/dynamic_update_slice | solution.py:350
  163.6 0.0 copy-start.2
  163.6 0.0 copy-start
  163.6 1.0 convert_bitcast_fusion
  164.6 0.5 copy-done.2
  165.1 1.0 copy.16
  166.1 0.0 copy-done
  166.1 1.2 copy.17
Async XLA Ops:
  7.2 154.0 %all-reduce.2.cloned.1.call-start = ((), (), s32[]{:S(2)}) async-start(), calls=%async_computation | async-start | bytes 458752 | tf_op jit(solution)/shard_map/psum | solution.py:342
  9.5 149.8 %copy-start.1 = (bf16[1,224,2048]{2,1,0:T(8,128)(2,1)S(1)}, bf16[1,224,2048]{2,1,0:T(8,128)(2,1)}, u32[]{:S(2)}) copy-start(bf16[1,224,2048]{2,1,0:T(8,128)(2,1)} %param.7) | copy-start | bytes 2752516
  163.6 1.6 copy-start.2
  163.6 2.5 %copy-start = (bf16[256,3584]{1,0:T(8,128)(2,1)S(1)}, bf16[256,3584]{1,0:T(8,128)(2,1)}, u32[]{:S(2)}) copy-start(bf16[256,3584]{1,0:T(8,128)(2,1)} %get-tuple-element.9) | copy-start | bytes 5505028
Sparse Core Ops, SparseCore 0:
  11.2 123.2 all-reduce.1

commit v2 on v1

--- a/solution.py
+++ b/solution.py
@@ -10,6 +10,8 @@
 
 KVW = 2048
 FRAGS = 4
+FRAGW = KVW // FRAGS
+REPLICAS = 16
 DW = 3584
 HALF = DW // 2
 TOK = 256
@@ -51,10 +53,12 @@
 
 
 def kernel(
-    hid_in, w_in, g_in, proj_out, ig_out, grad_out,
+    step_in, hid_in, w_in, g_in, global_in, moment_in,
+    proj_out, ig_out, weights_out, global_out, moment_out,
     hid, g_own, g_far, ht, n_halves, n_far, n_rows, wg, grads, ring,
-    back_own, back_send, back_far, p_own, p_send, p_far, igt, ig_rows, p_rows,
-    ag_send, ag_recv, rs_send, rs_recv, x_send, x_recv, local,
+    back_own, back_send, back_far, p_own, p_send, p_far, p_rows,
+    old_global, old_moment, frags, global_next, moment_next, new_rows,
+    ag_send, ag_recv, rs_send, rs_recv, x_send, x_recv, f_send, f_recv, local,
 ):
     replica = lax.axis_index("replica")
     place = lax.axis_index("fsdp")
@@ -62,6 +66,13 @@
     up = (replica, lax.rem(z + 1, NZ) * 2 + side)
     down = (replica, lax.rem(z + NZ - 1, NZ) * 2 + side)
     partner = (replica, z * 2 + 1 - side)
+    quad = lax.rem(replica, 4)
+    core_twin = (replica + 1 - 2 * lax.rem(replica, 2), place)
+    lane_twin = (replica - quad + lax.rem(quad + 2, 4), place)
+    columns = [(lax.rem(replica + 4 * k, 16), place) for k in range(1, 4)]
+    turn_now = lax.rem(step_in[0], FRAGS).astype(F32)
+    chosen = [1.0 - jnp.minimum(jnp.abs(turn_now - f), 1.0) for f in range(FRAGS)]
+    own_rows = pl.ds(pl.multiple_of(z * ROWS, 16), ROWS)
 
     def half_rows(block, d):
         return pl.ds(pl.multiple_of(block * ROWS + d * SIDE, 16), SIDE)
@@ -71,17 +82,20 @@
 
     load_hid = pltpu.make_async_copy(hid_in, hid, local.at[0])
     load_g = pltpu.make_async_copy(g_in, g_own, local.at[1])
-    load_w = pltpu.make_async_copy(
-        w_in, wg.at[pl.ds(pl.multiple_of(z * ROWS, 16), ROWS)], local.at[2]
-    )
+    load_w = pltpu.make_async_copy(w_in, wg.at[own_rows], local.at[2])
+    load_global = pltpu.make_async_copy(global_in, old_global, local.at[3])
+    load_moment = pltpu.make_async_copy(moment_in, old_moment, local.at[4])
+
+    barrier = pltpu.get_barrier_semaphore()
+    others = (up, down, partner, core_twin, lane_twin, *columns)
+    for other in others:
+        pl.semaphore_signal(barrier, inc=1, device_id=other, device_id_type=MESH)
     load_hid.start()
+    load_w.start()
     load_g.start()
-    load_w.start()
-
-    barrier = pltpu.get_barrier_semaphore()
-    for other in (up, down, partner):
-        pl.semaphore_signal(barrier, inc=1, device_id=other, device_id_type=MESH)
-    pl.semaphore_wait(barrier, 3)
+    load_global.start()
+    load_moment.start()
+    pl.semaphore_wait(barrier, len(others))
 
     def gather_copy(step, d):
         rows = half_rows(ring_block(step, d), d)
@@ -100,6 +114,13 @@
             device_id=partner, device_id_type=MESH,
         )
 
+    def frag_copy(src, dst, i, other):
+        return pltpu.make_async_remote_copy(
+            src_ref=frags.at[src], dst_ref=frags.at[dst],
+            send_sem=f_send.at[i], recv_sem=f_recv.at[i],
+            device_id=other, device_id_type=MESH,
+        )
+
     gathers = {}
 
     def gather_step(step):
@@ -109,6 +130,25 @@
             if step < NZ - 1:
                 gathers[step, d] = gather_copy(step, d)
                 gathers[step, d].start()
+
+    stores = []
+
+    def store(src, dst, i):
+        copy = pltpu.make_async_copy(src, dst, local.at[i])
+        copy.start()
+        stores.append(copy)
+
+    def new_weights(d, part, rows, total):
+        kept = pl.ds(d * SIDE, SIDE)
+        blend = global_next[kept, :]
+        for f in range(part * FRAGS // PARTS, (part + 1) * FRAGS // PARTS):
+            cols = pl.ds(f * FRAGW, FRAGW)
+            first = f * FRAGW - part * WIDE
+            updated = wg[rows, cols].astype(F32) - INNER_RATE * total[:, first : first + FRAGW]
+            keep = 1.0 - (1.0 - MIX_KEEP) * chosen[f]
+            new_rows[kept, cols] = (updated * keep + blend * (1.0 - keep)).astype(BF16)
+        cols = pl.ds(part * WIDE, WIDE)
+        store(new_rows.at[kept, cols], weights_out.at[kept, cols], 9 + part * 2 + d)
 
     sums = {}
 
@@ -125,7 +165,7 @@
                     slot = ring.at[d, step - 1, :, cols]
                     total = grads[rows, cols].astype(F32) + slot[...].astype(F32)
                     if step == NZ - 1:
-                        grad_out[pl.ds(d * SIDE, SIDE), cols] = total
+                        new_weights(d, part, rows, total)
                         continue
                     slot[...] = total.astype(BF16)
                     src = slot
@@ -165,9 +205,26 @@
     send_n = swap(n_halves.at[1 - side], n_far, 1)
     send_n.start()
 
+    def fragment(ref, rows):
+        return sum(
+            ref[rows, pl.ds(f * FRAGW, FRAGW)].astype(F32) * chosen[f] for f in range(FRAGS)
+        )
+
+    load_w.wait()
+    frags[0] = fragment(wg, own_rows).astype(BF16)
+    sent_frags = [frag_copy(0, 1, 0, core_twin)]
+    sent_frags[0].start()
+
     load_g.wait()
-    load_w.wait()
-    for step in range(1, 6):
+    gather_step(1)
+
+    gather_step(2)
+
+    sent_frags[0].wait_recv()
+    frags[2] = (frags[0].astype(F32) + frags[1].astype(F32)).astype(BF16)
+    sent_frags.append(frag_copy(2, 3, 1, lane_twin))
+    sent_frags[1].start()
+    for step in range(3, 6):
         gather_step(step)
 
     send_g.wait_recv()
@@ -194,6 +251,12 @@
 
     lax.fori_loop(0, HALF // 256, rows_of, 0)
     gather_step(7)
+
+    sent_frags[1].wait_recv()
+    frags[4] = (frags[2].astype(F32) + frags[3].astype(F32)).astype(BF16)
+    for k in range(3):
+        sent_frags.append(frag_copy(4, 5 + k, 2 + k, columns[k]))
+        sent_frags[2 + k].start()
 
     def back_tile(far):
         def run(i, _):
@@ -227,6 +290,20 @@
     sum_step(2)
     back_tile(False)
     sum_step(3)
+
+    load_global.wait()
+    load_moment.wait()
+    for k in range(3):
+        sent_frags[2 + k].wait_recv()
+    mean = frags[4].astype(F32)
+    for k in range(3):
+        mean = mean + frags[5 + k].astype(F32)
+    every = pl.ds(0, ROWS)
+    global_next[...], moment_next[...] = outer_update(
+        fragment(old_global, every), fragment(old_moment, every), mean * (1.0 / REPLICAS)
+    )
+    store(global_next, global_out, 5)
+    store(moment_next, moment_out, 6)
     project_tile(False)
     sum_step(4)
 
@@ -248,18 +325,17 @@
 
     def back_norm(i, _):
         for back, rows in row_pair(i):
-            igt[rows, :] = (back - ht[rows, :].astype(F32) * factor) * inverse
+            ht[rows, :] = ((back - ht[rows, :].astype(F32) * factor) * inverse).astype(BF16)
         return 0
 
     lax.fori_loop(0, NZ, back_norm, 0)
 
     def turn_back(i, _):
-        ig_rows[:, chunk(i, 256)] = igt[chunk(i, 256), :].T.astype(BF16)
+        hid[:, chunk(i, 256)] = ht[chunk(i, 256), :].astype(F32).T.astype(BF16)
         return 0
 
     lax.fori_loop(0, DW // 256, turn_back, 0)
-    store_ig = pltpu.make_async_copy(ig_rows, ig_out, local.at[3])
-    store_ig.start()
+    store(hid, ig_out, 7)
     sum_step(5)
 
     send_p.wait_recv()
@@ -270,14 +346,13 @@
         return 0
 
     lax.fori_loop(0, KVW // 512, finish, 0)
-    store_p = pltpu.make_async_copy(p_rows, proj_out, local.at[4])
-    store_p.start()
+    store(p_rows, proj_out, 8)
     sum_step(6)
     sum_step(7)
 
-    store_ig.wait()
-    store_p.wait()
-    for copy in (send_g, send_n, send_back, send_p):
+    for copy in stores:
+        copy.wait()
+    for copy in (send_g, send_n, send_back, send_p, *sent_frags):
         copy.wait_send()
     for copy in gathers.values():
         copy.wait_send()
@@ -285,7 +360,29 @@
         copy.wait_send()
 
 
-def step_kernel(hidden, weights, cot):
+def copy_kernel(*refs):
+    count = len(refs) // 2
+    copies = [
+        pltpu.make_async_copy(refs[i], refs[count + i], refs[-1].at[i]) for i in range(count)
+    ]
+    for copy in copies:
+        copy.start()
+    for copy in copies:
+        copy.wait()
+
+
+def copy_out(arrays):
+    anywhere = pl.BlockSpec(memory_space=pl.ANY)
+    return pl.pallas_call(
+        copy_kernel,
+        out_shape=tuple(jax.ShapeDtypeStruct(a.shape, a.dtype) for a in arrays),
+        in_specs=[pl.BlockSpec(memory_space=pltpu.VMEM)] * len(arrays),
+        out_specs=(anywhere,) * len(arrays),
+        scratch_shapes=[pltpu.SemaphoreType.DMA((len(arrays),))],
+    )(*arrays)
+
+
+def step_kernel(step, hidden, weights, cot, global_weights, moment):
     anywhere = pl.BlockSpec(memory_space=pl.ANY)
     vmem = pltpu.VMEM
     return pl.pallas_call(
@@ -293,10 +390,12 @@
         out_shape=(
             jax.ShapeDtypeStruct((TOK, KVW), BF16),
             jax.ShapeDtypeStruct((TOK, DW), BF16),
-            jax.ShapeDtypeStruct((ROWS, KVW), F32),
+            jax.ShapeDtypeStruct((ROWS, KVW), BF16),
+            jax.ShapeDtypeStruct((ROWS, FRAGW), F32),
+            jax.ShapeDtypeStruct((ROWS, FRAGW), F32),
         ),
-        in_specs=[anywhere] * 3,
-        out_specs=(anywhere, anywhere, pl.BlockSpec(memory_space=pltpu.VMEM)),
+        in_specs=[pl.BlockSpec(memory_space=pltpu.SMEM)] + [anywhere] * 5,
+        out_specs=(anywhere,) * 5,
         scratch_shapes=[
             vmem((TOK, DW), BF16),
             vmem((TOK, KVW), BF16),
@@ -314,9 +413,13 @@
             vmem((TOK, KVW), F32),
             vmem((TOK, KVW), BF16),
             vmem((TOK, KVW), BF16),
-            vmem((DW, TOK), F32),
-            vmem((TOK, DW), BF16),
             vmem((TOK, KVW), BF16),
+            vmem((ROWS, KVW), F32),
+            vmem((ROWS, KVW), F32),
+            vmem((8, ROWS, FRAGW), BF16),
+            vmem((ROWS, FRAGW), F32),
+            vmem((ROWS, FRAGW), F32),
+            vmem((ROWS, KVW), BF16),
             pltpu.SemaphoreType.DMA((2, NZ - 1)),
             pltpu.SemaphoreType.DMA((2, NZ - 1)),
             pltpu.SemaphoreType.DMA((2, PARTS, NZ - 1)),
@@ -324,6 +427,8 @@
             pltpu.SemaphoreType.DMA((4,)),
             pltpu.SemaphoreType.DMA((4,)),
             pltpu.SemaphoreType.DMA((5,)),
+            pltpu.SemaphoreType.DMA((5,)),
+            pltpu.SemaphoreType.DMA((9 + 2 * PARTS,)),
         ],
         compiler_params=pltpu.CompilerParams(
             collective_id=0, has_side_effects=True, vmem_limit_bytes=56 << 20
@@ -331,23 +436,14 @@
         cost_estimate=pl.CostEstimate(
             flops=6 * TOK * DW * KVW, bytes_accessed=600 << 20, transcendentals=0
         ),
-    )(hidden, weights, cot)
+    )(step, hidden, weights, cot, global_weights, moment)
 
 
 def body(hidden_in, local_weights, cotangent, global_weights, outer_momentum, step_index):
-    frag_cols = KVW // FRAGS
-    start = step_index[0] % FRAGS * frag_cols
-    local_frag = lax.dynamic_slice_in_dim(local_weights[0], start, frag_cols, 1)
-    replicas = lax.axis_size("replica")
-    total = lax.psum(local_frag, "replica").astype(F32)
-    projected, input_grad, gradient = step_kernel(hidden_in[0], local_weights[0], cotangent[0])
-    global_frag = lax.dynamic_slice_in_dim(global_weights, start, frag_cols, 1)
-    moment_frag = lax.dynamic_slice_in_dim(outer_momentum, start, frag_cols, 1)
-    new_global, new_momentum = outer_update(global_frag, moment_frag, total / replicas)
-    updated = local_weights[0].astype(F32) - INNER_RATE * gradient
-    upd_frag = lax.dynamic_slice_in_dim(updated, start, frag_cols, 1)
-    mixed = MIX_KEEP * upd_frag + (1.0 - MIX_KEEP) * new_global
-    new_weights = lax.dynamic_update_slice_in_dim(updated, mixed, start, 1).astype(BF16)
+    results = step_kernel(
+        step_index, hidden_in[0], local_weights[0], cotangent[0], global_weights, outer_momentum
+    )
+    projected, input_grad, new_weights, new_global, new_momentum = copy_out(results)
     return (projected[None], input_grad[None], new_weights[None], new_global, new_momentum)
 
 

time: 175 us -> 157 us (0.90)
  between operations: 14.7 us -> 1.29 us
  other arithmetic: 5.21 us -> 0 us
  Pallas kernels: 150 us -> 155 us
  local copies, waits for them, and re-layouts: 4.36 us -> 0 us
    pallas_call x0 -> x1, Pallas kernels: none -> 4.51 us  [copy_out(): pl.pallas_call(copy_kernel, out_shape=tuple((jax.ShapeDtypeStruct(a.shape...]
    unnamed x8 -> x0, local copies, waits for them, and re-layouts: 2.71 us -> none
    dynamic_update_slice x1 -> x0, other arithmetic: 2.43 us -> none  [body(): lax.dynamic_update_slice_in_dim(updated, mixed, start, 1).astype(BF16)]
  transfers between devices with their start and end apart: 1 -> 0, of which waited for: 0 -> 0; matrix products, arithmetic and copies ran while one was open for 1% -> 0% of each run, Pallas kernels for 86% -> 0%
where the time goes in v2:
time: 157 us
  Pallas kernels  155 us (99%)
    pallas_call x1, Pallas kernels, step_kernel(): pl.pallas_call(kernel, out_shape=(jax.ShapeDtypeStruct((TOK, KVW), BF16),...  151 us
    pallas_call x1, Pallas kernels, copy_out(): pl.pallas_call(copy_kernel, out_shape=tuple((jax.ShapeDtypeStruct(a.shape...  4.51 us

profile of v2, /device:TPU:2, one launch (start us, length us, event | category | flops | bytes accessed | tf_op | source)
XLA Modules:
  0.0 156.6 jit_solution(11992090335877394375)
XLA Ops:
  1.3 150.8 %shard_map.101 = (bf16[256,2048]{1,0:T(8,128)(2,1)}, bf16[256,3584]{1,0:T(8,128)(2,1)}, bf16[224,2048]{1,0:T(8,128)(2,1)}, f32[224,512]{1,0:T(8,128)}, f32[224,512]{1,0:T(8,128)}) custom-call(s32[1]{0:T(128)S(6)} %copy.11.step_in, bf16[256,3584]{1,0:T(8,128)(2,1)} %bitcast.6, bf16[224,2048]{1,0:T(8,128)(2,1)} %bitcast.10, bf16[256,2048]{1,0:T(8,128)(2,1)} %bitcast.8, ...), custom_call_target="tpu_custom_call" | custom-call | flops 11274289152 | bytes 629145600 | tf_op jit(solution)/shard_map/pallas_call | solution.py:388
  152.0 4.5 %shard_map.102 = (bf16[256,2048]{1,0:T(8,128)(2,1)}, bf16[256,3584]{1,0:T(8,128)(2,1)}, bf16[224,2048]{1,0:T(8,128)(2,1)}, f32[224,512]{1,0:T(8,128)}, f32[224,512]{1,0:T(8,128)}) custom-call(bf16[256,2048]{1,0:T(8,128)(2,1)} %get-tuple-element.15.refs_0_, bf16[256,3584]{1,0:T(8,128)(2,1)} %get-tuple-element.16.refs_1_, ...), custom_call_target="tpu_custom_call" | custom-call | tf_op jit(solution)/shard_map/pallas_call | solution.py:376

commit v3 on v2

--- a/solution.py
+++ b/solution.py
@@ -56,8 +56,8 @@
     step_in, hid_in, w_in, g_in, global_in, moment_in,
     proj_out, ig_out, weights_out, global_out, moment_out,
     hid, g_own, g_far, ht, n_halves, n_far, n_rows, wg, grads, ring,
-    back_own, back_send, back_far, p_own, p_send, p_far, p_rows,
-    old_global, old_moment, frags, global_next, moment_next, new_rows,
+    step, back_own, back_send, back_far, p_own, p_send, p_far,
+    old_global, old_moment, frags,
     ag_send, ag_recv, rs_send, rs_recv, x_send, x_recv, f_send, f_recv, local,
 ):
     replica = lax.axis_index("replica")
@@ -70,8 +70,6 @@
     core_twin = (replica + 1 - 2 * lax.rem(replica, 2), place)
     lane_twin = (replica - quad + lax.rem(quad + 2, 4), place)
     columns = [(lax.rem(replica + 4 * k, 16), place) for k in range(1, 4)]
-    turn_now = lax.rem(step_in[0], FRAGS).astype(F32)
-    chosen = [1.0 - jnp.minimum(jnp.abs(turn_now - f), 1.0) for f in range(FRAGS)]
     own_rows = pl.ds(pl.multiple_of(z * ROWS, 16), ROWS)
 
     def half_rows(block, d):
@@ -80,6 +78,8 @@
     def ring_block(step, d):
         return lax.rem(z - step + 2 * NZ, NZ) if d == 0 else lax.rem(z + step, NZ)
 
+    load_step = pltpu.make_async_copy(step_in, step, local.at[5])
+    load_step.start()
     load_hid = pltpu.make_async_copy(hid_in, hid, local.at[0])
     load_g = pltpu.make_async_copy(g_in, g_own, local.at[1])
     load_w = pltpu.make_async_copy(w_in, wg.at[own_rows], local.at[2])
@@ -97,13 +97,13 @@
     load_moment.start()
     pl.semaphore_wait(barrier, len(others))
 
-    def gather_copy(step, d):
-        rows = half_rows(ring_block(step, d), d)
+    def gather_copy(step, d, part):
+        rows, cols = half_rows(ring_block(step, d), d), pl.ds(part * WIDE, WIDE)
         return pltpu.make_async_remote_copy(
-            src_ref=w_in.at[pl.ds(d * SIDE, SIDE)] if step == 0 else wg.at[rows],
-            dst_ref=wg.at[rows],
-            send_sem=ag_send.at[d, step],
-            recv_sem=ag_recv.at[d, step],
+            src_ref=w_in.at[pl.ds(d * SIDE, SIDE), cols] if step == 0 else wg.at[rows, cols],
+            dst_ref=wg.at[rows, cols],
+            send_sem=ag_send.at[d, part, step],
+            recv_sem=ag_recv.at[d, part, step],
             device_id=up if d == 0 else down,
             device_id_type=MESH,
         )
@@ -124,31 +124,23 @@
     gathers = {}
 
     def gather_step(step):
-        for d in range(2):
-            if step > 0:
-                gathers[step - 1, d].wait_recv()
-            if step < NZ - 1:
-                gathers[step, d] = gather_copy(step, d)
-                gathers[step, d].start()
-
-    stores = []
-
-    def store(src, dst, i):
-        copy = pltpu.make_async_copy(src, dst, local.at[i])
-        copy.start()
-        stores.append(copy)
+        for part in range(PARTS):
+            for d in range(2):
+                if step > 0:
+                    gathers[step - 1, d, part].wait_recv()
+                if step < NZ - 1:
+                    gathers[step, d, part] = gather_copy(step, d, part)
+                    gathers[step, d, part].start()
 
     def new_weights(d, part, rows, total):
         kept = pl.ds(d * SIDE, SIDE)
-        blend = global_next[kept, :]
+        blend = global_out[kept, :]
         for f in range(part * FRAGS // PARTS, (part + 1) * FRAGS // PARTS):
             cols = pl.ds(f * FRAGW, FRAGW)
             first = f * FRAGW - part * WIDE
             updated = wg[rows, cols].astype(F32) - INNER_RATE * total[:, first : first + FRAGW]
             keep = 1.0 - (1.0 - MIX_KEEP) * chosen[f]
-            new_rows[kept, cols] = (updated * keep + blend * (1.0 - keep)).astype(BF16)
-        cols = pl.ds(part * WIDE, WIDE)
-        store(new_rows.at[kept, cols], weights_out.at[kept, cols], 9 + part * 2 + d)
+            weights_out[kept, cols] = (updated * keep + blend * (1.0 - keep)).astype(BF16)
 
     sums = {}
 
@@ -205,6 +197,10 @@
     send_n = swap(n_halves.at[1 - side], n_far, 1)
     send_n.start()
 
+    load_step.wait()
+    turn_now = lax.rem(step[0], FRAGS).astype(F32)
+    chosen = [1.0 - jnp.minimum(jnp.abs(turn_now - f), 1.0) for f in range(FRAGS)]
+
     def fragment(ref, rows):
         return sum(
             ref[rows, pl.ds(f * FRAGW, FRAGW)].astype(F32) * chosen[f] for f in range(FRAGS)
@@ -299,11 +295,9 @@
     for k in range(3):
         mean = mean + frags[5 + k].astype(F32)
     every = pl.ds(0, ROWS)
-    global_next[...], moment_next[...] = outer_update(
+    global_out[...], moment_out[...] = outer_update(
         fragment(old_global, every), fragment(old_moment, every), mean * (1.0 / REPLICAS)
     )
-    store(global_next, global_out, 5)
-    store(moment_next, moment_out, 6)
     project_tile(False)
     sum_step(4)
 
@@ -331,27 +325,23 @@
     lax.fori_loop(0, NZ, back_norm, 0)
 
     def turn_back(i, _):
-        hid[:, chunk(i, 256)] = ht[chunk(i, 256), :].astype(F32).T.astype(BF16)
+        ig_out[:, chunk(i, 256)] = ht[chunk(i, 256), :].astype(F32).T.astype(BF16)
         return 0
 
     lax.fori_loop(0, DW // 256, turn_back, 0)
-    store(hid, ig_out, 7)
     sum_step(5)
 
     send_p.wait_recv()
 
     def finish(i, _):
         cols = chunk(i, 512)
-        p_rows[:, cols] = (p_own[:, cols] + p_far[:, cols].astype(F32)).astype(BF16)
+        proj_out[:, cols] = (p_own[:, cols] + p_far[:, cols].astype(F32)).astype(BF16)
         return 0
 
     lax.fori_loop(0, KVW // 512, finish, 0)
-    store(p_rows, proj_out, 8)
     sum_step(6)
     sum_step(7)
 
-    for copy in stores:
-        copy.wait()
     for copy in (send_g, send_n, send_back, send_p, *sent_frags):
         copy.wait_send()
     for copy in gathers.values():
@@ -379,6 +369,7 @@
         in_specs=[pl.BlockSpec(memory_space=pltpu.VMEM)] * len(arrays),
         out_specs=(anywhere,) * len(arrays),
         scratch_shapes=[pltpu.SemaphoreType.DMA((len(arrays),))],
+        compiler_params=pltpu.CompilerParams(vmem_limit_bytes=2 << 20),
     )(*arrays)
 
 
@@ -388,14 +379,14 @@
     return pl.pallas_call(
         kernel,
         out_shape=(
-            jax.ShapeDtypeStruct((TOK, KVW), BF16),
-            jax.ShapeDtypeStruct((TOK, DW), BF16),
-            jax.ShapeDtypeStruct((ROWS, KVW), BF16),
-            jax.ShapeDtypeStruct((ROWS, FRAGW), F32),
-            jax.ShapeDtypeStruct((ROWS, FRAGW), F32),
+            vmem((TOK, KVW), BF16),
+            vmem((TOK, DW), BF16),
+            vmem((ROWS, KVW), BF16),
+            vmem((ROWS, FRAGW), F32),
+            vmem((ROWS, FRAGW), F32),
         ),
-        in_specs=[pl.BlockSpec(memory_space=pltpu.SMEM)] + [anywhere] * 5,
-        out_specs=(anywhere,) * 5,
+        in_specs=[pl.BlockSpec(memory_space=pltpu.HBM)] + [anywhere] * 5,
+        out_specs=(pl.BlockSpec(memory_space=pltpu.VMEM),) * 5,
         scratch_shapes=[
             vmem((TOK, DW), BF16),
             vmem((TOK, KVW), BF16),
@@ -407,31 +398,28 @@
             vmem((HALF, KVW), BF16),
             vmem((HALF, KVW), BF16),
             vmem((2, NZ - 1, SIDE, KVW), BF16),
+            pltpu.SMEM((1,), jnp.int32),
             vmem((HALF, TOK), F32),
             vmem((HALF, TOK), BF16),
             vmem((HALF, TOK), BF16),
             vmem((TOK, KVW), F32),
             vmem((TOK, KVW), BF16),
             vmem((TOK, KVW), BF16),
-            vmem((TOK, KVW), BF16),
             vmem((ROWS, KVW), F32),
             vmem((ROWS, KVW), F32),
             vmem((8, ROWS, FRAGW), BF16),
-            vmem((ROWS, FRAGW), F32),
-            vmem((ROWS, FRAGW), F32),
-            vmem((ROWS, KVW), BF16),
-            pltpu.SemaphoreType.DMA((2, NZ - 1)),
-            pltpu.SemaphoreType.DMA((2, NZ - 1)),
+            pltpu.SemaphoreType.DMA((2, PARTS, NZ - 1)),
+            pltpu.SemaphoreType.DMA((2, PARTS, NZ - 1)),
             pltpu.SemaphoreType.DMA((2, PARTS, NZ - 1)),
             pltpu.SemaphoreType.DMA((2, PARTS, NZ - 1)),
             pltpu.SemaphoreType.DMA((4,)),
             pltpu.SemaphoreType.DMA((4,)),
             pltpu.SemaphoreType.DMA((5,)),
             pltpu.SemaphoreType.DMA((5,)),
-            pltpu.SemaphoreType.DMA((9 + 2 * PARTS,)),
+            pltpu.SemaphoreType.DMA((6,)),
         ],
         compiler_params=pltpu.CompilerParams(
-            collective_id=0, has_side_effects=True, vmem_limit_bytes=56 << 20
+            collective_id=0, has_side_effects=True, vmem_limit_bytes=54 << 20
         ),
         cost_estimate=pl.CostEstimate(
             flops=6 * TOK * DW * KVW, bytes_accessed=600 << 20, transcendentals=0

time: 157 us -> 153 us (0.975)
  Pallas kernels: 155 us -> 151 us
    pallas_call x1, Pallas kernels: 4.51 us -> 2.22 us  [copy_out(): pl.pallas_call(copy_kernel, out_shape=tuple((jax.ShapeDtypeStruct(a.shape...]
    pallas_call x1, Pallas kernels: 151 us -> 149 us  [step_kernel(): pl.pallas_call(kernel, out_shape=(vmem((TOK, KVW), BF16), vmem((TOK, DW),...]
where the time goes in v3:
time: 153 us
  Pallas kernels  151 us (99%)
    pallas_call x1, Pallas kernels, step_kernel(): pl.pallas_call(kernel, out_shape=(vmem((TOK, KVW), BF16), vmem((TOK, DW),...  149 us

profile of v3, /device:TPU:2, one launch (start us, length us, event | category | flops | bytes accessed | tf_op | source)
XLA Modules:
  0.0 152.6 jit_solution(12431228128031157591)
XLA Ops:
  1.3 149.1 %shard_map.101 = (bf16[256,2048]{1,0:T(8,128)(2,1)S(1)}, bf16[256,3584]{1,0:T(8,128)(2,1)S(1)}, bf16[224,2048]{1,0:T(8,128)(2,1)S(1)}, f32[224,512]{1,0:T(8,128)S(1)}, f32[224,512]{1,0:T(8,128)S(1)}) custom-call(s32[1]{0:T(128)S(6)} %copy.11.step_in, bf16[256,3584]{1,0:T(8,128)(2,1)} %bitcast.6, bf16[224,2048]{1,0:T(8,128)(2,1)} %bitcast.10, ...), custom_call_target="tpu_custom_call" | custom-call | flops 11274289152 | bytes 629145600 | tf_op jit(solution)/shard_map/pallas_call | solution.py:379
  150.4 2.2 %shard_map.102 = (bf16[256,2048]{1,0:T(8,128)(2,1)}, bf16[256,3584]{1,0:T(8,128)(2,1)}, bf16[224,2048]{1,0:T(8,128)(2,1)}, f32[224,512]{1,0:T(8,128)}, f32[224,512]{1,0:T(8,128)}) custom-call(bf16[256,2048]{1,0:T(8,128)(2,1)S(1)} %get-tuple-element.15.refs_0_, bf16[256,3584]{1,0:T(8,128)(2,1)S(1)} %get-tuple-element.16.refs_1_, ...), custom_call_target="tpu_custom_call" | custom-call | tf_op jit(solution)/shard_map/pallas_call | solution.py:366

commit v4 on v3

--- a/solution.py
+++ b/solution.py
@@ -132,15 +132,20 @@
                     gathers[step, d, part] = gather_copy(step, d, part)
                     gathers[step, d, part].start()
 
-    def new_weights(d, part, rows, total):
+    def begin_weights():
+        for f in range(FRAGS):
+            cols = pl.ds(f * FRAGW, FRAGW)
+            keep = 1.0 - (1.0 - MIX_KEEP) * chosen[f]
+            own = wg[own_rows, cols].astype(F32) - INNER_RATE * grads[own_rows, cols].astype(F32)
+            old_global[:, cols] = own * keep + global_out[...] * (1.0 - keep)
+
+    def end_weights(d, part):
         kept = pl.ds(d * SIDE, SIDE)
-        blend = global_out[kept, :]
         for f in range(part * FRAGS // PARTS, (part + 1) * FRAGS // PARTS):
             cols = pl.ds(f * FRAGW, FRAGW)
-            first = f * FRAGW - part * WIDE
-            updated = wg[rows, cols].astype(F32) - INNER_RATE * total[:, first : first + FRAGW]
-            keep = 1.0 - (1.0 - MIX_KEEP) * chosen[f]
-            weights_out[kept, cols] = (updated * keep + blend * (1.0 - keep)).astype(BF16)
+            rate = INNER_RATE * (1.0 - (1.0 - MIX_KEEP) * chosen[f])
+            last = ring[d, NZ - 2, :, cols].astype(F32)
+            weights_out[kept, cols] = (old_global[kept, cols] - rate * last).astype(BF16)
 
     sums = {}
 
@@ -154,11 +159,11 @@
                     src = grads.at[rows, cols]
                 else:
                     sums[step - 1, d, part].wait_recv()
+                    if step == NZ - 1:
+                        end_weights(d, part)
+                        continue
                     slot = ring.at[d, step - 1, :, cols]
                     total = grads[rows, cols].astype(F32) + slot[...].astype(F32)
-                    if step == NZ - 1:
-                        new_weights(d, part, rows, total)
-                        continue
                     slot[...] = total.astype(BF16)
                     src = slot
                 sums[step, d, part] = pltpu.make_async_remote_copy(
@@ -339,15 +344,20 @@
         return 0
 
     lax.fori_loop(0, KVW // 512, finish, 0)
+    begin_weights()
     sum_step(6)
-    sum_step(7)
-
     for copy in (send_g, send_n, send_back, send_p, *sent_frags):
         copy.wait_send()
     for copy in gathers.values():
         copy.wait_send()
-    for copy in sums.values():
-        copy.wait_send()
+    for (step, _, _), copy in sums.items():
+        if step < NZ - 2:
+            copy.wait_send()
+    sum_step(7)
+
+    for (step, _, _), copy in sums.items():
+        if step == NZ - 2:
+            copy.wait_send()
 
 
 def copy_kernel(*refs):

time: 153 us -> 152 us (level)
  no operation moved by 1% of the time
where the time goes in v4:
time: 152 us
  Pallas kernels  151 us (99%)
    pallas_call x1, Pallas kernels, step_kernel(): pl.pallas_call(kernel, out_shape=(vmem((TOK, KVW), BF16), vmem((TOK, DW),...  149 us

profile of v4, /device:TPU:2, one launch (start us, length us, event | category | flops | bytes accessed | tf_op | source)
XLA Modules:
  0.0 152.4 jit_solution(16780835788183528055)
XLA Ops:
  1.3 148.9 %shard_map.101 = (bf16[256,2048]{1,0:T(8,128)(2,1)S(1)}, bf16[256,3584]{1,0:T(8,128)(2,1)S(1)}, bf16[224,2048]{1,0:T(8,128)(2,1)S(1)}, f32[224,512]{1,0:T(8,128)S(1)}, f32[224,512]{1,0:T(8,128)S(1)}) custom-call(s32[1]{0:T(128)S(6)} %copy.11.step_in, bf16[256,3584]{1,0:T(8,128)(2,1)} %bitcast.6, bf16[224,2048]{1,0:T(8,128)(2,1)} %bitcast.10, ...), custom_call_target="tpu_custom_call" | custom-call | flops 11274289152 | bytes 629145600 | tf_op jit(solution)/shard_map/pallas_call | solution.py:389
  150.1 2.2 %shard_map.102 = (bf16[256,2048]{1,0:T(8,128)(2,1)}, bf16[256,3584]{1,0:T(8,128)(2,1)}, bf16[224,2048]{1,0:T(8,128)(2,1)}, f32[224,512]{1,0:T(8,128)}, f32[224,512]{1,0:T(8,128)}) custom-call(bf16[256,2048]{1,0:T(8,128)(2,1)S(1)} %get-tuple-element.15.refs_0_, bf16[256,3584]{1,0:T(8,128)(2,1)S(1)} %get-tuple-element.16.refs_1_, ...), custom_call_target="tpu_custom_call" | custom-call | tf_op jit(solution)/shard_map/pallas_call | solution.py:376

commit v5 on v4

--- a/solution.py
+++ b/solution.py
@@ -70,6 +70,10 @@
     core_twin = (replica + 1 - 2 * lax.rem(replica, 2), place)
     lane_twin = (replica - quad + lax.rem(quad + 2, 4), place)
     columns = [(lax.rem(replica + 4 * k, 16), place) for k in range(1, 4)]
+    barrier = pltpu.get_barrier_semaphore()
+    others = (up, down, partner, core_twin, lane_twin, *columns)
+    for other in others:
+        pl.semaphore_signal(barrier, inc=1, device_id=other, device_id_type=MESH)
     own_rows = pl.ds(pl.multiple_of(z * ROWS, 16), ROWS)
 
     def half_rows(block, d):
@@ -79,22 +83,15 @@
         return lax.rem(z - step + 2 * NZ, NZ) if d == 0 else lax.rem(z + step, NZ)
 
     load_step = pltpu.make_async_copy(step_in, step, local.at[5])
-    load_step.start()
     load_hid = pltpu.make_async_copy(hid_in, hid, local.at[0])
     load_g = pltpu.make_async_copy(g_in, g_own, local.at[1])
     load_w = pltpu.make_async_copy(w_in, wg.at[own_rows], local.at[2])
     load_global = pltpu.make_async_copy(global_in, old_global, local.at[3])
     load_moment = pltpu.make_async_copy(moment_in, old_moment, local.at[4])
 
-    barrier = pltpu.get_barrier_semaphore()
-    others = (up, down, partner, core_twin, lane_twin, *columns)
-    for other in others:
-        pl.semaphore_signal(barrier, inc=1, device_id=other, device_id_type=MESH)
+    load_step.start()
     load_hid.start()
     load_w.start()
-    load_g.start()
-    load_global.start()
-    load_moment.start()
     pl.semaphore_wait(barrier, len(others))
 
     def gather_copy(step, d, part):
@@ -179,6 +176,9 @@
     gather_step(0)
     send_g = swap(g_in, g_far, 0)
     send_g.start()
+    load_g.start()
+    load_global.start()
+    load_moment.start()
 
     load_hid.wait()
 
@@ -365,8 +365,8 @@
     copies = [
         pltpu.make_async_copy(refs[i], refs[count + i], refs[-1].at[i]) for i in range(count)
     ]
-    for copy in copies:
-        copy.start()
+    for i in (1, 0, 2, 3, 4):
+        copies[i].start()
     for copy in copies:
         copy.wait()
 

time: 152 us -> 152 us (level)
  no operation moved by 1% of the time
where the time goes in v5:
time: 152 us
  Pallas kernels  151 us (99%)
    pallas_call x1, Pallas kernels, step_kernel(): pl.pallas_call(kernel, out_shape=(vmem((TOK, KVW), BF16), vmem((TOK, DW),...  149 us

profile of v5, /device:TPU:2, one launch (start us, length us, event | category | flops | bytes accessed | tf_op | source)
XLA Modules:
  0.0 152.4 jit_solution(4275368955315762402)
XLA Ops:
  1.3 148.9 %shard_map.101 = (bf16[256,2048]{1,0:T(8,128)(2,1)S(1)}, bf16[256,3584]{1,0:T(8,128)(2,1)S(1)}, bf16[224,2048]{1,0:T(8,128)(2,1)S(1)}, f32[224,512]{1,0:T(8,128)S(1)}, f32[224,512]{1,0:T(8,128)S(1)}) custom-call(s32[1]{0:T(128)S(6)} %copy.11.step_in, bf16[256,3584]{1,0:T(8,128)(2,1)} %bitcast.6, bf16[224,2048]{1,0:T(8,128)(2,1)} %bitcast.10, ...), custom_call_target="tpu_custom_call" | custom-call | flops 11274289152 | bytes 629145600 | tf_op jit(solution)/shard_map/pallas_call | solution.py:389
  150.1 2.2 %shard_map.102 = (bf16[256,2048]{1,0:T(8,128)(2,1)}, bf16[256,3584]{1,0:T(8,128)(2,1)}, bf16[224,2048]{1,0:T(8,128)(2,1)}, f32[224,512]{1,0:T(8,128)}, f32[224,512]{1,0:T(8,128)}) custom-call(bf16[256,2048]{1,0:T(8,128)(2,1)S(1)} %get-tuple-element.15.refs_0_, bf16[256,3584]{1,0:T(8,128)(2,1)S(1)} %get-tuple-element.16.refs_1_, ...), custom_call_target="tpu_custom_call" | custom-call | tf_op jit(solution)/shard_map/pallas_call | solution.py:376

commit v6 on v5

--- a/solution.py
+++ b/solution.py
@@ -18,6 +18,7 @@
 ROWS = 224
 SIDE = ROWS // 2
 NZ = 8
+HOPS = NZ // 2
 PARTS = 2
 WIDE = KVW // PARTS
 SCALE = 1.0 / math.sqrt(DW)
@@ -94,13 +95,20 @@
     load_w.start()
     pl.semaphore_wait(barrier, len(others))
 
-    def gather_copy(step, d, part):
-        rows, cols = half_rows(ring_block(step, d), d), pl.ds(part * WIDE, WIDE)
+    def chunks(step, d, last):
+        for half in (d, 1 - d):
+            if step == last and half != d:
+                continue
+            for part in range(PARTS):
+                yield half, part, pl.ds(part * WIDE, WIDE)
+
+    def gather_copy(step, d, half, part):
+        rows, cols = half_rows(ring_block(step, d), half), pl.ds(part * WIDE, WIDE)
         return pltpu.make_async_remote_copy(
-            src_ref=w_in.at[pl.ds(d * SIDE, SIDE), cols] if step == 0 else wg.at[rows, cols],
+            src_ref=w_in.at[pl.ds(half * SIDE, SIDE), cols] if step == 0 else wg.at[rows, cols],
             dst_ref=wg.at[rows, cols],
-            send_sem=ag_send.at[d, part, step],
-            recv_sem=ag_recv.at[d, part, step],
+            send_sem=ag_send.at[d, half, part, step],
+            recv_sem=ag_recv.at[d, half, part, step],
             device_id=up if d == 0 else down,
             device_id_type=MESH,
         )
@@ -121,13 +129,18 @@
     gathers = {}
 
     def gather_step(step):
-        for part in range(PARTS):
+        for k in range(2 * PARTS):
             for d in range(2):
                 if step > 0:
-                    gathers[step - 1, d, part].wait_recv()
-                if step < NZ - 1:
-                    gathers[step, d, part] = gather_copy(step, d, part)
-                    gathers[step, d, part].start()
+                    arrived = list(chunks(step - 1, d, HOPS - 1))
+                    if k < len(arrived):
+                        half, part, _ = arrived[k]
+                        gathers[step - 1, d, half, part].wait_recv()
+                leaving = list(chunks(step, d, HOPS - 1)) if step < HOPS else []
+                if k < len(leaving):
+                    half, part, _ = leaving[k]
+                    gathers[step, d, half, part] = gather_copy(step, d, half, part)
+                    gathers[step, d, half, part].start()
 
     def begin_weights():
         for f in range(FRAGS):
@@ -136,42 +149,48 @@
             own = wg[own_rows, cols].astype(F32) - INNER_RATE * grads[own_rows, cols].astype(F32)
             old_global[:, cols] = own * keep + global_out[...] * (1.0 - keep)
 
-    def end_weights(d, part):
-        kept = pl.ds(d * SIDE, SIDE)
-        for f in range(part * FRAGS // PARTS, (part + 1) * FRAGS // PARTS):
-            cols = pl.ds(f * FRAGW, FRAGW)
-            rate = INNER_RATE * (1.0 - (1.0 - MIX_KEEP) * chosen[f])
-            last = ring[d, NZ - 2, :, cols].astype(F32)
-            weights_out[kept, cols] = (old_global[kept, cols] - rate * last).astype(BF16)
-
     sums = {}
 
+    def sum_send(step, d, half, part, cols, src):
+        sums[step, d, half, part] = pltpu.make_async_remote_copy(
+            src_ref=src,
+            dst_ref=ring.at[d, step, half, :, cols],
+            send_sem=rs_send.at[d, half, part, step],
+            recv_sem=rs_recv.at[d, half, part, step],
+            device_id=up if d == 0 else down,
+            device_id_type=MESH,
+        )
+        sums[step, d, half, part].start()
+
     def sum_step(step):
-        for part in range(PARTS):
-            cols = pl.ds(part * WIDE, WIDE)
+        for k in range(2 * PARTS):
             for d in range(2):
-                block = ring_block(step + 1, d)
-                rows = half_rows(block, d)
-                if step == 0:
-                    src = grads.at[rows, cols]
-                else:
-                    sums[step - 1, d, part].wait_recv()
-                    if step == NZ - 1:
-                        end_weights(d, part)
-                        continue
-                    slot = ring.at[d, step - 1, :, cols]
+                todo = list(chunks(step, d, 0))
+                if k >= len(todo):
+                    continue
+                half, part, cols = todo[k]
+                rows = half_rows(ring_block(step + HOPS, d), half)
+                if (step - 1, d, half, part) in sums:
+                    sums[step - 1, d, half, part].wait_recv()
+                    slot = ring.at[d, step - 1, half, :, cols]
                     total = grads[rows, cols].astype(F32) + slot[...].astype(F32)
                     slot[...] = total.astype(BF16)
-                    src = slot
-                sums[step, d, part] = pltpu.make_async_remote_copy(
-                    src_ref=src,
-                    dst_ref=ring.at[d, step, :, cols],
-                    send_sem=rs_send.at[d, part, step],
-                    recv_sem=rs_recv.at[d, part, step],
-                    device_id=up if d == 0 else down,
-                    device_id_type=MESH,
-                )
-                sums[step, d, part].start()
+                    sum_send(step, d, half, part, cols, slot)
+                else:
+                    sum_send(step, d, half, part, cols, grads.at[rows, cols])
+
+    def sum_end():
+        last = HOPS - 1
+        for k in range(2 * PARTS):
+            half, part = k % 2, k // 2
+            for d in (half, 1 - half):
+                sums[last, d, half, part].wait_recv()
+            kept = pl.ds(half * SIDE, SIDE)
+            for f in range(part * FRAGS // PARTS, (part + 1) * FRAGS // PARTS):
+                cols = pl.ds(f * FRAGW, FRAGW)
+                rate = INNER_RATE * (1.0 - (1.0 - MIX_KEEP) * chosen[f])
+                total = ring[0, last, half, :, cols].astype(F32) + ring[1, last, half, :, cols].astype(F32)
+                weights_out[kept, cols] = (old_global[kept, cols] - rate * total).astype(BF16)
 
     gather_step(0)
     send_g = swap(g_in, g_far, 0)
@@ -219,14 +238,11 @@
     load_g.wait()
     gather_step(1)
 
-    gather_step(2)
-
     sent_frags[0].wait_recv()
     frags[2] = (frags[0].astype(F32) + frags[1].astype(F32)).astype(BF16)
     sent_frags.append(frag_copy(2, 3, 1, lane_twin))
     sent_frags[1].start()
-    for step in range(3, 6):
-        gather_step(step)
+    gather_step(2)
 
     send_g.wait_recv()
     send_n.wait_recv()
@@ -241,7 +257,7 @@
         return 0
 
     lax.fori_loop(0, HALF // 256, gradient_tile, 0)
-    gather_step(6)
+    gather_step(3)
     sum_step(0)
 
     def rows_of(i, _):
@@ -251,7 +267,7 @@
         return 0
 
     lax.fori_loop(0, HALF // 256, rows_of, 0)
-    gather_step(7)
+    gather_step(4)
 
     sent_frags[1].wait_recv()
     frags[4] = (frags[2].astype(F32) + frags[3].astype(F32)).astype(BF16)
@@ -284,13 +300,12 @@
     back_tile(True)
     send_back = swap(back_send, back_far, 2)
     send_back.start()
-    sum_step(1)
     project_tile(True)
     send_p = swap(p_send, p_far, 3)
     send_p.start()
-    sum_step(2)
+    sum_step(1)
     back_tile(False)
-    sum_step(3)
+    project_tile(False)
 
     load_global.wait()
     load_moment.wait()
@@ -304,7 +319,7 @@
         fragment(old_global, every), fragment(old_moment, every), mean * (1.0 / REPLICAS)
     )
     project_tile(False)
-    sum_step(4)
+    sum_step(2)
 
     send_back.wait_recv()
 
@@ -334,7 +349,7 @@
         return 0
 
     lax.fori_loop(0, DW // 256, turn_back, 0)
-    sum_step(5)
+    sum_step(3)
 
     send_p.wait_recv()
 
@@ -345,18 +360,16 @@
 
     lax.fori_loop(0, KVW // 512, finish, 0)
     begin_weights()
-    sum_step(6)
     for copy in (send_g, send_n, send_back, send_p, *sent_frags):
         copy.wait_send()
     for copy in gathers.values():
         copy.wait_send()
-    for (step, _, _), copy in sums.items():
-        if step < NZ - 2:
+    for (step, _, _, _), copy in sums.items():
+        if step < HOPS - 1:
             copy.wait_send()
-    sum_step(7)
-
-    for (step, _, _), copy in sums.items():
-        if step == NZ - 2:
+    sum_end()
+    for (step, _, _, _), copy in sums.items():
+        if step == HOPS - 1:
             copy.wait_send()
 
 
@@ -407,7 +420,7 @@
             vmem((2, TOK, HALF), BF16),
             vmem((HALF, KVW), BF16),
             vmem((HALF, KVW), BF16),
-            vmem((2, NZ - 1, SIDE, KVW), BF16),
+            vmem((2, HOPS, 2, SIDE, KVW), BF16),
             pltpu.SMEM((1,), jnp.int32),
             vmem((HALF, TOK), F32),
             vmem((HALF, TOK), BF16),
@@ -418,10 +431,10 @@
             vmem((ROWS, KVW), F32),
             vmem((ROWS, KVW), F32),
             vmem((8, ROWS, FRAGW), BF16),
-            pltpu.SemaphoreType.DMA((2, PARTS, NZ - 1)),
-            pltpu.SemaphoreType.DMA((2, PARTS, NZ - 1)),
-            pltpu.SemaphoreType.DMA((2, PARTS, NZ - 1)),
-            pltpu.SemaphoreType.DMA((2, PARTS, NZ - 1)),
+            pltpu.SemaphoreType.DMA((2, 2, PARTS, HOPS)),
+            pltpu.SemaphoreType.DMA((2, 2, PARTS, HOPS)),
+            pltpu.SemaphoreType.DMA((2, 2, PARTS, HOPS)),
+            pltpu.SemaphoreType.DMA((2, 2, PARTS, HOPS)),
             pltpu.SemaphoreType.DMA((4,)),
             pltpu.SemaphoreType.DMA((4,)),
             pltpu.SemaphoreType.DMA((5,)),
@@ -429,7 +442,7 @@
             pltpu.SemaphoreType.DMA((6,)),
         ],
         compiler_params=pltpu.CompilerParams(
-            collective_id=0, has_side_effects=True, vmem_limit_bytes=54 << 20
+            collective_id=0, has_side_effects=True, vmem_limit_bytes=55 << 20
         ),
         cost_estimate=pl.CostEstimate(
             flops=6 * TOK * DW * KVW, bytes_accessed=600 << 20, transcendentals=0

time: 152 us -> 153 us (level)
  no operation moved by 1% of the time
where the time goes in v6:
time: 153 us; the launch traced here: 152 us
  Pallas kernels  151 us (99%)
    pallas_call x1, Pallas kernels, step_kernel(): pl.pallas_call(kernel, out_shape=(vmem((TOK, KVW), BF16), vmem((TOK, DW),...  149 us

profile of v6, /device:TPU:2, one launch (start us, length us, event | category | flops | bytes accessed | tf_op | source)
XLA Modules:
  0.0 152.5 jit_solution(17006970431828140782)
XLA Ops:
  1.3 149.0 %shard_map.101 = (bf16[256,2048]{1,0:T(8,128)(2,1)S(1)}, bf16[256,3584]{1,0:T(8,128)(2,1)S(1)}, bf16[224,2048]{1,0:T(8,128)(2,1)S(1)}, f32[224,512]{1,0:T(8,128)S(1)}, f32[224,512]{1,0:T(8,128)S(1)}) custom-call(s32[1]{0:T(128)S(6)} %copy.11.step_in, bf16[256,3584]{1,0:T(8,128)(2,1)} %bitcast.6, bf16[224,2048]{1,0:T(8,128)(2,1)} %bitcast.10, ...), custom_call_target="tpu_custom_call" | custom-call | flops 11274289152 | bytes 629145600 | tf_op jit(solution)/shard_map/pallas_call | solution.py:402
  150.3 2.2 %shard_map.102 = (bf16[256,2048]{1,0:T(8,128)(2,1)}, bf16[256,3584]{1,0:T(8,128)(2,1)}, bf16[224,2048]{1,0:T(8,128)(2,1)}, f32[224,512]{1,0:T(8,128)}, f32[224,512]{1,0:T(8,128)}) custom-call(bf16[256,2048]{1,0:T(8,128)(2,1)S(1)} %get-tuple-element.15.refs_0_, bf16[256,3584]{1,0:T(8,128)(2,1)S(1)} %get-tuple-element.16.refs_1_, ...), custom_call_target="tpu_custom_call" | custom-call | tf_op jit(solution)/shard_map/pallas_call | solution.py:389
